TPU v7x, 32 devices: a whole 2x2x4 slice. The times are simulated.
32 devices in a mesh: groups: 2 (over y), member: 4 (over x, core), grid: 4 (over z).
Axes of the slice: x: 2, y: 2, z: 4, core: 2. Of those that a mesh axis runs over, the one named last changes fastest.
Arguments:
- latent: bfloat16 [8, 256, 1024], P(('groups', 'member'), 'grid'), parts along dimension 0, may hold values from -6 to 6
- w_message: bfloat16 [1024, 1024], replicated, may hold values from -0.1875 to 0.1875
- edge_embed: float32 [4, 1024], replicated, may hold values from -3 to 3
- w_node: bfloat16 [1024, 1024], replicated, may hold values from -0.1875 to 0.1875
- w_output: bfloat16 [100, 1024], replicated, may hold values from -0.1875 to 0.1875
- send_list: int32 [4, 4, 8], P('grid'), may hold values from 0 to 63, as said below
- edge_src: int32 [3, 4096], P(None, 'grid'), may hold values from 0 to 31, as said below
- edge_feat: float32 [4, 3, 4096], P(None, None, 'grid'), may hold values from -6 to 6
- cell_area: float32 [4096], P('grid'), may hold values from 0.3 to 3
- target: bfloat16 [100, 8192], P(None, ('groups', 'grid')), parts along dimension 1, may hold values from -6 to 6
Outputs:
- latent_grad: bfloat16 [8, 256, 1024], P(('groups', 'member'), 'grid'), parts along dimension 0
- point_score: float32 [8192], P(('groups', 'grid')), parts along dimension 0
There are 2 independent parts, one for each index of `groups`. A program takes and returns all parts, laid end to end along the dimension named above; an argument that names none is the same for every part. Nothing has to cross between parts.
Inputs may be any that keep to these rules, and one draw needn't show every extreme that they name: send_list[s, b, j] is a row among the 64 mesh nodes owned by block s; entries may repeat. edge_src[k, g] = s * 8 + j names slot j of the rows that owner s sends to the block holding grid point g.
All inputs are finite; a program needn't handle non-finite values.
Results may differ from a plain program's by a relative error of at most 0.0062.
Values may be sent and summed in bfloat16 or wider, within the bound.
A program may use at most 64 MiB of HBM per device.

v0:
```python
import jax
import jax.numpy as jnp
from jax import lax
from jax.sharding import PartitionSpec as P

K = 3


softness = 0.1


def silu_slope(value):
    sigma = jax.nn.sigmoid(value)
    return sigma * (1.0 + value * (1.0 - sigma))


def smooth_abs(value):
    return jnp.sqrt(value * value + softness * softness)


def smooth_slope(value):
    return value / smooth_abs(value)


def edge_terms(features, edge_embed, which):
    total = features[0, which, :][:, None] * edge_embed[0][None, :]
    for feature in range(1, features.shape[0]):
        total = total + features[feature, which, :][:, None] * edge_embed[feature][None, :]
    return total


def pick_table(indices, count, dtype):
    return (indices[:, None] == jnp.arange(count, dtype=jnp.int32)[None, :]).astype(dtype)


def decode_forward(received, sources, features, edge_embed, w_node, w_output):
    summed = jnp.zeros((sources.shape[1], received.shape[1]), jnp.float32)
    for edge in range(K):
        looked = jnp.take(received, sources[edge], axis=0).astype(jnp.float32)
        pre_act = looked + edge_terms(features, edge_embed, edge)
        summed = summed + jax.nn.silu(pre_act)
    hidden = (summed / K).astype(jnp.bfloat16)
    mixed = jnp.dot(hidden, w_node, preferred_element_type=jnp.float32)
    outer = (hidden.astype(jnp.float32) + jax.nn.silu(mixed)).astype(jnp.bfloat16)
    predicted = lax.dot_general(
        w_output, outer, (((1,), (1,)), ((), ())), preferred_element_type=jnp.float32
    ).astype(jnp.bfloat16)
    return (predicted, mixed)


def decode_backward(received, sources, features, edge_embed, w_node, w_output, mixed, grad_pred):
    slot_total = received.shape[0]
    grad_outer = lax.dot_general(
        grad_pred, w_output, (((0,), (0,)), ((), ())), preferred_element_type=jnp.float32
    )
    grad_mixed = (grad_outer * silu_slope(mixed)).astype(jnp.bfloat16)
    grad_hidden = grad_outer + lax.dot_general(
        grad_mixed, w_node, (((1,), (1,)), ((), ())), preferred_element_type=jnp.float32
    )
    grad_summed = grad_hidden / K
    slot_grad = jnp.zeros(received.shape, jnp.float32)
    for edge in range(K):
        looked = jnp.take(received, sources[edge], axis=0).astype(jnp.float32)
        pre_act = looked + edge_terms(features, edge_embed, edge)
        edge_grad = (grad_summed * silu_slope(pre_act)).astype(jnp.bfloat16)
        table = pick_table(sources[edge], slot_total, jnp.bfloat16)
        slot_grad = slot_grad + lax.dot_general(
            table, edge_grad, (((0,), (0,)), ((), ())), preferred_element_type=jnp.float32
        )
    return slot_grad


def score_terms(ensemble, truth, cell_area):
    members = ensemble.shape[0]
    skill = jnp.zeros(truth.shape, jnp.float32)
    spread = jnp.zeros(truth.shape, jnp.float32)
    for member in range(members):
        skill = skill + smooth_abs(ensemble[member] - truth)
        spread = spread + jnp.sum(smooth_abs(ensemble[member][None] - ensemble), axis=0)
    spread = spread - members * softness
    crps = skill / members - spread / (2.0 * members * (members - 1))
    return cell_area * jnp.mean(crps, axis=0)


def slope_terms(own, ensemble, truth, cell_area):
    members = ensemble.shape[0]
    pairs = jnp.zeros(own.shape, jnp.float32)
    for member in range(members):
        pairs = pairs + smooth_slope(own - ensemble[member])
    return cell_area * (smooth_slope(own - truth) / members - pairs / (members * (members - 1)))


def per_device(
    latent,
    w_message,
    edge_embed,
    w_node,
    w_output,
    send_list,
    edge_src,
    edge_feat,
    cell_area,
    target,
):
    owners = lax.axis_size("grid")
    mesh_rows = latent[0]
    send_rows = send_list[0]
    slot_count = send_rows.shape[1]
    width = mesh_rows.shape[1]
    own_count = mesh_rows.shape[0]
    flat_sends = send_rows.reshape(-1)
    send_table = pick_table(flat_sends, own_count, jnp.bfloat16)
    projected = jnp.dot(mesh_rows, w_message, preferred_element_type=jnp.float32).astype(
        jnp.bfloat16
    )
    outgoing = (
        jnp.dot(send_table, projected, preferred_element_type=jnp.float32)
        .astype(jnp.bfloat16)
        .reshape(owners, slot_count, width)
    )
    incoming = lax.all_to_all(outgoing, "grid", split_axis=0, concat_axis=0, tiled=True)
    received = incoming.reshape(owners * slot_count, width)
    predicted, mixed = decode_forward(received, edge_src, edge_feat, edge_embed, w_node, w_output)
    truth = target.astype(jnp.float32)
    ensemble = lax.all_gather(predicted[None], "member", axis=0, tiled=True).astype(jnp.float32)
    point_score = score_terms(ensemble, truth, cell_area)
    grad_pred = slope_terms(predicted.astype(jnp.float32), ensemble, truth, cell_area).astype(
        jnp.bfloat16
    )
    slot_grad = decode_backward(
        received, edge_src, edge_feat, edge_embed, w_node, w_output, mixed, grad_pred
    )
    slot_low = slot_grad.astype(jnp.bfloat16).reshape(owners, slot_count, width)
    returned = lax.all_to_all(slot_low, "grid", split_axis=0, concat_axis=0, tiled=True)
    row_grad = lax.dot_general(
        send_table,
        returned.reshape(-1, width),
        (((0,), (0,)), ((), ())),
        preferred_element_type=jnp.float32,
    )
    latent_grad = lax.dot_general(
        row_grad.astype(jnp.bfloat16),
        w_message,
        (((1,), (1,)), ((), ())),
        preferred_element_type=jnp.float32,
    ).astype(jnp.bfloat16)
    return (latent_grad[None], point_score)


def solution(mesh):
    return jax.shard_map(
        per_device,
        mesh=mesh,
        in_specs=(
            P(("groups", "member"), "grid", None),
            P(),
            P(),
            P(),
            P(),
            P("grid", None, None),
            P(None, "grid"),
            P(None, None, "grid"),
            P("grid"),
            P(None, ("groups", "grid")),
        ),
        out_specs=(P(("groups", "member"), "grid", None), P(("groups", "grid"))),
        check_vma=False,
    )
```

profile of v0, /device:TPU:0, one launch (start us, length us, event | category | flops | bytes accessed | tf_op | source)
XLA Modules:
  0.0 84.3 jit_solution(5669110157921758032)
XLA Ops:
  0.6 0.0 copy-start
  0.6 0.9 %eq.56 = s32[32]{0:T(128)S(1)} reshape(s32[1,4,8]{2,1,0:T(4,128)} %param.17) | data formatting | bytes 256 | tf_op jit(solution)/shard_map/eq | solution.py:33
  1.6 2.9 %fusion.28 = bf16[4,8,1024]{2,1,0:T(8,128)(2,1)} fusion(bf16[1024,1024]{1,0:T(8,128)(2,1)} %param.13, bf16[1,64,1024]{2,1,0:T(8,128)(2,1)} %param.12, s32[32]{0:T(128)S(1)} %eq.56), kind=kOutput, calls=%fused_computation.55 | convolution fusion | flops 138512384 | bytes 2293888 | tf_op jit(solution)/shard_map/dot_general | solution.py:117
  4.5 6.3 %all-to-all-start = ((bf16[4,8,1024]{2,1,0:T(8,128)(2,1)}), bf16[4,8,1024]{2,1,0:T(8,128)(2,1)S(1)}, u32[]{:S(2)}, u32[]{:S(2)}) async-start(bf16[4,8,1024]{2,1,0:T(8,128)(2,1)} %fusion.28), calls=%async_computation | async-start | bytes 131072 | tf_op jit(solution)/shard_map/all_to_all | solution.py:121
  10.8 0.8 fusion.79
  11.7 0.9 %fusion.80 = (f32[1,1024]{1,0:T(1,128)S(1)}, f32[1,1024]{1,0:T(1,128)S(1)}, f32[1,1024]{1,0:T(1,128)S(1)}, f32[1,1024]{1,0:T(1,128)S(1)}) fusion(f32[4,1024]{1,0:T(4,128)} %param.14), kind=kLoop, calls=%fused_computation.129 | loop fusion | bytes 32768 | tf_op jit(solution)/shard_map/slice | solution.py:26
  12.6 1.0 %fusion.78 = (f32[1,1,1024]{2,0,1:T(1,128)S(1)}, f32[1,1,1024]{2,0,1:T(1,128)S(1)}, f32[1,1,1024]{2,0,1:T(1,128)S(1)}, f32[1,1,1024]{2,0,1:T(1,128)S(1)}, f32[1,...) fusion(f32[4,3,1024]{2,0,1:T(4,128)} %param.19), kind=kLoop, calls=%fused_computation.127 | loop fusion | bytes 98304 | tf_op jit(solution)/shard_map/slice | solution.py:26
  13.6 2.9 %all-to-all-done = bf16[4,8,1024]{2,1,0:T(8,128)(2,1)S(1)} async-done(((bf16[4,8,1024]{2,1,0:T(8,128)(2,1)}), bf16[4,8,1024]{2,1,0:T(8,128)(2,1)S(1)}, u32[]{:S(2)}, u32[]{:S(2)}) %all-to-all-start) | async-done | bytes 65568 | tf_op jit(solution)/shard_map/all_to_all | solution.py:121
  16.5 5.3 %gather_fusion.2 = bf16[1024,1024]{1,0:T(8,128)(2,1)} fusion(bf16[32,1024]{1,0:T(8,128)(2,1)S(1)} %bitcast.76, s32[1024]{0:T(1024)S(1)} %fusion.66), kind=kCustom, calls=%fused_computation.2.clone | custom fusion | bytes 4198400 | tf_op jit(solution)/shard_map/jit(_take)/gather | solution.py:39
  21.9 5.3 %gather_fusion.1 = bf16[1024,1024]{1,0:T(8,128)(2,1)} fusion(bf16[32,1024]{1,0:T(8,128)(2,1)S(1)} %bitcast.77, s32[1024]{0:T(1024)S(1)} %fusion.65), kind=kCustom, calls=%fused_computation.1.clone | custom fusion | bytes 4198400 | tf_op jit(solution)/shard_map/jit(_take)/gather | solution.py:39
  27.2 5.3 %gather_fusion = bf16[1024,1024]{1,0:T(8,128)(2,1)} fusion(bf16[32,1024]{1,0:T(8,128)(2,1)S(1)} %bitcast.78, s32[1024]{0:T(1024)S(1)} %fusion.64), kind=kCustom, calls=%fused_computation.clone | custom fusion | bytes 4198400 | tf_op jit(solution)/shard_map/jit(_take)/gather | solution.py:39
  32.5 9.7 %multiply_convert_fusion.4 = bf16[1024,1024]{1,0:T(8,128)(2,1)S(1)} fusion(f32[1024]{0:T(1024)S(1)} %bitcast.93, f32[1024]{0:T(1024)S(1)} %bitcast.95, f32[1024]{0:T(1024)S(1)} %bitcast.89, f32[1024]{0:T(1024)S(1)} %bitcast.91, f32[1024]{0:T(1024)S(1)} %bitcast.97, f32[1024]{0:T(1024)S(1)} %bitcast.99, f32[1024]{0:T(1024)S(1)} %bitcast.101, ...), kind=kLoop, calls=%fused_computation.10 | loop fusion | flops 48234496 | bytes 8457216 | tf_op jit(solution)/shard_map/convert_element_type | solution.py:42
  42.2 0.0 copy-done
  42.2 0.0 copy-start.8
  42.2 2.4 %fusion.81 = f32[1024,1024]{1,0:T(8,128)S(1)} fusion(bf16[1024,1024]{1,0:T(8,128)(2,1)S(1)} %multiply_convert_fusion.4, bf16[1024,1024]{1,0:T(8,128)(2,1)S(1)} %copy-done), kind=kOutput, calls=%fused_computation.130 | convolution fusion | flops 2147483648 | bytes 8388608 | tf_op jit(solution)/shard_map/dot_general | solution.py:43
  44.6 0.0 copy-done.8
  44.6 1.3 %fusion.21 = bf16[1024,100]{0,1:T(8,128)(2,1)S(1)} fusion(bf16[100,1024]{1,0:T(8,128)(2,1)S(1)} %copy-done.8, f32[1024,1024]{1,0:T(8,128)S(1)} %fusion.81, bf16[1024,1024]{1,0:T(8,128)(2,1)S(1)} %multiply_convert_fusion.4), kind=kOutput, calls=%fused_computation.45 | convolution fusion | flops 217157632 | bytes 6701056 | tf_op jit(solution)/shard_map/dot_general | solution.py:45
  45.9 0.0 copy-start.6
  45.9 0.0 copy-start.9
  45.9 9.3 %all-gather.1 = bf16[4,100,1024]{2,1,0:T(8,128)(2,1)S(1)} all-gather(bf16[1,100,1024]{2,1,0:T(8,128)(2,1)S(1)} %bitcast.79), channel_id=2, replica_groups=mesh['groups'=2,'member'=4,'grid'=4] {'member'}, dimensions={0}, use_global_device_ids=true | all-gather | bytes 1024000 | tf_op jit(solution)/shard_map/all_gather | solution.py:125
  55.2 0.2 convert_element_type.92
  55.4 0.0 copy-start.1
  55.4 1.3 %slice_bitcast_fusion.1 = (f32[100,1024]{1,0:T(8,128)S(1)}, f32[100,1024]{1,0:T(8,128)}, f32[100,1024]{1,0:T(8,128)}, f32[100,1024]{1,0:T(8,128)}) fusion(f32[4,100,1024]{2,1,0:T(8,128)S(1)} %convert_element_type.92), kind=kLoop, calls=%fused_computation.87 | loop fusion | bytes 3276800 | tf_op jit(solution)/shard_map/slice | solution.py:89
  56.7 0.3 copy-done.1
  57.0 0.0 copy-done.6
  57.0 0.0 copy-done.9
  57.0 1.1 %fusion.51 = f32[1024,1024]{1,0:T(8,128)S(1)} fusion(bf16[100,1024]{1,0:T(8,128)(2,1)S(1)} %copy-done.8, bf16[100,1024]{1,0:T(8,128)(2,1)S(1)} %copy-done.6, bf16[1024,100]{0,1:T(8,128)(2,1)S(1)} %fusion.21, f32[1024]{0:T(1024)S(1)} %copy-done.9, f32[4,100,1024]{2,1,0:T(8,128)S(1)} %convert_element_type.92), kind=kOutput, calls=%fused_computation.95 | convolution fusion | flops 212787200 | bytes 6451200 | tf_op jit(solution)/shard_map/dot_general | solution.py:53
  58.1 0.0 copy-start.5
  58.1 3.2 %add_multiply_fusion = f32[1024,1024]{1,0:T(8,128)S(1)} fusion(f32[1024,1024]{1,0:T(8,128)S(1)} %fusion.51, bf16[1024,1024]{1,0:T(8,128)(2,1)S(1)} %copy-done, f32[1024,1024]{1,0:T(8,128)S(1)} %fusion.81), kind=kOutput, calls=%fused_computation.6 | convolution fusion | flops 2159017984 | bytes 14680064 | tf_op jit(solution)/shard_map/dot_general | solution.py:57
  61.3 0.0 copy-done.5
  61.4 0.0 copy-start.4
  61.4 3.1 %fusion.2 = f32[32,1024]{1,0:T(8,128)S(1)} fusion(f32[1024,1024]{1,0:T(8,128)S(1)} %add_multiply_fusion, f32[1024]{0:T(1024)S(1)} %bitcast.122, f32[1024]{0:T(1024)S(1)} %bitcast.108, f32[1024]{0:T(1024)S(1)} %bitcast.126, f32[1024]{0:T(1024)S(1)} %bitcast.110, f32[1024]{0:T(1024)S(1)} %bitcast.118, f32[1024]{0:T(1024)S(1)} %bitcast.112, ...), kind=kOutput, calls=%fused_computation.22 | convolution fusion | flops 87064576 | bytes 6460416 | tf_op jit(solution)/shard_map/dot_general | solution.py:67
  64.5 0.0 copy-done.4
  64.5 0.0 copy-start.3
  64.5 3.1 %fusion.25 = f32[32,1024]{1,0:T(8,128)S(1)} fusion(f32[32,1024]{1,0:T(8,128)S(1)} %fusion.2, f32[1024,1024]{1,0:T(8,128)S(1)} %add_multiply_fusion, f32[1024]{0:T(1024)S(1)} %bitcast.98, f32[1024]{0:T(1024)S(1)} %bitcast.100, f32[1024]{0:T(1024)S(1)} %bitcast.102, f32[1024]{0:T(1024)S(1)} %bitcast.104, f32[1024]{0:T(1024)S(1)} %bitcast.123, ...), kind=kOutput, calls=%fused_computation.52 | convolution fusion | flops 87097344 | bytes 6591488 | tf_op jit(solution)/shard_map/dot_general | solution.py:67
  67.6 0.0 copy-done.3
  67.6 4.0 %fusion.29 = bf16[4,8,1024]{2,1,0:T(8,128)(2,1)} fusion(f32[32,1024]{1,0:T(8,128)S(1)} %fusion.25, f32[1024,1024]{1,0:T(8,128)S(1)} %add_multiply_fusion, f32[1024]{0:T(1024)S(1)} %bitcast.94, f32[1024]{0:T(1024)S(1)} %bitcast.96, f32[1024]{0:T(1024)S(1)} %bitcast.90, f32[1024]{0:T(1024)S(1)} %bitcast.92, f32[1024]{0:T(1024)S(1)} %bitcast.124, ...), kind=kOutput, calls=%fused_computation.56 | convolution fusion | flops 87130112 | bytes 6525952 | tf_op jit(solution)/shard_map/dot_general | solution.py:67
  71.6 3.3 %all-to-all-start.1 = ((bf16[4,8,1024]{2,1,0:T(8,128)(2,1)}), bf16[4,8,1024]{2,1,0:T(8,128)(2,1)S(1)}, u32[]{:S(2)}, u32[]{:S(2)}) async-start(bf16[4,8,1024]{2,1,0:T(8,128)(2,1)} %fusion.29), calls=%async_computation.1 | async-start | bytes 131072 | tf_op jit(solution)/shard_map/all_to_all | solution.py:134
  74.9 0.0 copy-start.2
  74.9 0.0 copy-start.7
  74.9 4.9 %fusion.20 = (f32[100,1024]{1,0:T(8,128)S(1)}, f32[100,1024]{1,0:T(8,128)S(1)}, f32[100,1024]{1,0:T(8,128)S(1)}, f32[100,1024]{1,0:T(8,128)S(1)}) fusion(bf16[4,100,1024]{2,1,0:T(8,128)(2,1)S(1)} %all-gather.1, f32[100,1024]{1,0:T(8,128)} %get-tuple-element.8, f32[100,1024]{1,0:T(8,128)} %get-tuple-element.9, f32[100,1024]{1,0:T(8,128)} %get-tuple-element.10, ...), kind=kLoop, calls=%fused_computation.44 | loop fusion | flops 6553600 | bytes 4096000 | tf_op jit(solution)/shard_map/reduce_sum | solution.py:79
  79.8 0.0 copy-done.2
  79.8 0.0 copy-done.7
  79.8 0.7 fusion.47
  80.5 0.6 multiply_multiply_fusion
  81.1 0.0 all-to-all-done.1
  81.1 3.2 %fusion.23 = bf16[1,64,1024]{2,1,0:T(8,128)(2,1)} fusion(bf16[1024,1024]{1,0:T(8,128)(2,1)} %param.13, bf16[4,8,1024]{2,1,0:T(8,128)(2,1)S(1)} %all-to-all-done.1, s32[32]{0:T(128)S(1)} %eq.56), kind=kOutput, calls=%fused_computation.50 | convolution fusion | flops 138545152 | bytes 2293888 | tf_op jit(solution)/shard_map/dot_general | solution.py:141
  (5 shorter events, 0.0 us)
Async XLA Ops:
  0.6 41.5 %copy-start = (bf16[1024,1024]{1,0:T(8,128)(2,1)S(1)}, bf16[1024,1024]{1,0:T(8,128)(2,1)}, u32[]{:S(2)}) copy-start(bf16[1024,1024]{1,0:T(8,128)(2,1)} %param.15) | copy-start | bytes 6291460
  4.5 12.1 %all-to-all-start = ((bf16[4,8,1024]{2,1,0:T(8,128)(2,1)}), bf16[4,8,1024]{2,1,0:T(8,128)(2,1)S(1)}, u32[]{:S(2)}, u32[]{:S(2)}) async-start(bf16[4,8,1024]{2,1,0:T(8,128)(2,1)} %fusion.28), calls=%async_computation | async-start | bytes 131072 | tf_op jit(solution)/shard_map/all_to_all | solution.py:121
  42.2 2.4 %copy-start.8 = (bf16[100,1024]{1,0:T(8,128)(2,1)S(1)}, bf16[100,1024]{1,0:T(8,128)(2,1)}, u32[]{:S(2)}) copy-start(bf16[100,1024]{1,0:T(8,128)(2,1)} %param.16) | copy-start | bytes 614404
  45.9 11.1 %copy-start.6 = (bf16[100,1024]{1,0:T(8,128)(2,1)S(1)}, bf16[100,1024]{1,0:T(8,128)(2,1)}, u32[]{:S(2)}) copy-start(bf16[100,1024]{1,0:T(8,128)(2,1)} %param.21) | copy-start | bytes 614404
  45.9 11.1 %copy-start.9 = (f32[1024]{0:T(1024)S(1)}, f32[1024]{0:T(1024)}, u32[]{:S(2)}) copy-start(f32[1024]{0:T(1024)} %param.20) | copy-start | bytes 12292
  55.4 1.6 %copy-start.1 = (f32[4,100,1024]{2,1,0:T(8,128)}, f32[4,100,1024]{2,1,0:T(8,128)S(1)}, u32[]{:S(2)}) copy-start(f32[4,100,1024]{2,1,0:T(8,128)S(1)} %convert_element_type.92) | copy-start | bytes 4915204
  58.1 3.2 %copy-start.5 = (bf16[1024,1024]{1,0:T(8,128)(2,1)S(1)}, bf16[1024,1024]{1,0:T(8,128)(2,1)}, u32[]{:S(2)}) copy-start(bf16[1024,1024]{1,0:T(8,128)(2,1)} %gather_fusion) | copy-start | bytes 6291460
  61.4 3.2 %copy-start.4 = (bf16[1024,1024]{1,0:T(8,128)(2,1)S(1)}, bf16[1024,1024]{1,0:T(8,128)(2,1)}, u32[]{:S(2)}) copy-start(bf16[1024,1024]{1,0:T(8,128)(2,1)} %gather_fusion.1) | copy-start | bytes 6291460
  64.5 3.1 %copy-start.3 = (bf16[1024,1024]{1,0:T(8,128)(2,1)S(1)}, bf16[1024,1024]{1,0:T(8,128)(2,1)}, u32[]{:S(2)}) copy-start(bf16[1024,1024]{1,0:T(8,128)(2,1)} %gather_fusion.2) | copy-start | bytes 6291460
  71.6 9.5 %all-to-all-start.1 = ((bf16[4,8,1024]{2,1,0:T(8,128)(2,1)}), bf16[4,8,1024]{2,1,0:T(8,128)(2,1)S(1)}, u32[]{:S(2)}, u32[]{:S(2)}) async-start(bf16[4,8,1024]{2,1,0:T(8,128)(2,1)} %fusion.29), calls=%async_computation.1 | async-start | bytes 131072 | tf_op jit(solution)/shard_map/all_to_all | solution.py:134
  74.9 4.9 %copy-start.2 = (f32[4,100,1024]{2,1,0:T(8,128)S(1)}, f32[4,100,1024]{2,1,0:T(8,128)}, u32[]{:S(2)}) copy-start(f32[4,100,1024]{2,1,0:T(8,128)} %copy-done.1) | copy-start | bytes 4915204
  74.9 4.9 %copy-start.7 = (bf16[100,1024]{1,0:T(8,128)(2,1)S(1)}, bf16[100,1024]{1,0:T(8,128)(2,1)}, u32[]{:S(2)}) copy-start(bf16[100,1024]{1,0:T(8,128)(2,1)} %param.21) | copy-start | bytes 614404
where the time goes:
time: 85.1 us; the launch traced here: 84.3 us
  matrix products  24.3 us (29%)
  local copies, waits for them, and re-layouts  21.3 us (25%)
  other arithmetic  16.1 us (19%)
  starting transfers between devices  9.6 us (11%)
  blocking collectives  9.26 us (11%)
  waiting for transfers between devices  2.94 us (3%)
  between operations  0.89 us (1%)
    gather x3, local copies, waits for them, and re-layouts, decode_forward(): looked = jnp.take(received, sources[edge], axis=0).astype(jnp.float32)  16 us
    dot_general x3, matrix products, decode_backward(): lax.dot_general(table, edge_grad, (((0,), (0,)), ((), ())), preferred_ele...  10.2 us
    convert_element_type x1, other arithmetic, decode_forward(): hidden = (summed / K).astype(jnp.bfloat16)  9.66 us
    all_gather x1, blocking collectives, per_device(): lax.all_gather(predicted[None], 'member', axis=0, tiled=True)  9.26 us
    all_to_all x1, starting transfers between devices, per_device(): lax.all_to_all(outgoing, 'grid', split_axis=0, concat_axis=0, tiled=True)  6.32 us
    reduce_sum x1, other arithmetic, score_terms(): jnp.sum(smooth_abs(ensemble[member][None] - ensemble), axis=0)  4.86 us
    all_to_all x1, starting transfers between devices, per_device(): lax.all_to_all(slot_low, 'grid', split_axis=0, concat_axis=0, tiled=True)  3.28 us
    dot_general x1, matrix products, per_device(): lax.dot_general(row_grad.astype(jnp.bfloat16), w_message, (((1,), (1,)),...  3.2 us
  transfers between devices with their start and end apart: 2, of which 1 were waited for; matrix products, arithmetic and copies ran while one was open for 11% of the time, Pallas kernels for 0%

commit v1 on v0

v1 whole, which is shorter than its diff:
```python
import functools

import jax
import jax.numpy as jnp
from jax import lax
from jax.experimental import pallas as pl
from jax.experimental.pallas import tpu as pltpu
from jax.sharding import PartitionSpec as P

F32 = jnp.float32
BF16 = jnp.bfloat16
MESH = pl.DeviceIdType.MESH

softness = 0.1
CHUNK = 256
TILE = 256


def rup(value, unit):
    return (value + unit - 1) // unit * unit


def nt_dot(a, b):
    return lax.dot_general(a, b, (((1,), (1,)), ((), ())), preferred_element_type=F32)


def tn_dot(a, b):
    return lax.dot_general(a, b, (((0,), (0,)), ((), ())), preferred_element_type=F32)


def nn_dot(a, b):
    return jnp.dot(a, b, preferred_element_type=F32)


def kernel(
    members,
    owners,
    latent_ref,
    wm_hbm,
    embed_ref,
    wn_hbm,
    wo_ref,
    sends_ref,
    src_ref,
    feat_ref,
    area_ref,
    target_ref,
    grad_ref,
    score_ref,
    wm,
    wn,
    table,
    outgoing,
    received,
    back,
    returned,
    picks,
    picks_t,
    terms,
    low,
    hid,
    outr,
    edge_slope,
    mix_slope,
    go_scr,
    gm_scr,
    ens,
    slot,
    local_sem,
    out_send,
    out_recv,
    back_send,
    back_recv,
    cross_send,
    cross_recv,
    sib_send,
    sib_recv,
):
    width = latent_ref.shape[2]
    nodes = latent_ref.shape[1]
    edges, points = src_ref.shape
    feats = feat_ref.shape[0]
    slots = sends_ref.shape[2]
    variables = wo_ref.shape[0]
    rows_in = owners * slots
    chunks = points // CHUNK
    tiles = [slice(t, t + TILE) for t in range(0, width, TILE)]
    pairs = members // 2

    zi = lax.axis_index("grid")
    mi = lax.axis_index("member")
    hi, lo = lax.div(mi, 2), lax.rem(mi, 2)
    sibling = hi * 2 + 1 - lo

    load_wm = pltpu.make_async_copy(wm_hbm, wm, local_sem.at[0])
    load_wn = pltpu.make_async_copy(wn_hbm, wn, local_sem.at[1])
    load_wm.start()
    load_wn.start()

    def grid_peer(step):
        return lax.rem(zi + step, owners)

    def member_peer(step):
        return lax.rem(hi + step, pairs) * 2 + lo

    barrier = pltpu.get_barrier_semaphore()
    for step in range(1, owners):
        pl.semaphore_signal(
            barrier, inc=1, device_id={"grid": grid_peer(step)}, device_id_type=MESH
        )
    for step in range(1, pairs):
        pl.semaphore_signal(
            barrier, inc=1, device_id={"member": member_peer(step)}, device_id_type=MESH
        )
    pl.semaphore_signal(barrier, inc=1, device_id={"member": sibling}, device_id_type=MESH)

    eye = lax.broadcasted_iota(jnp.int32, (slots, slots), 0) == lax.broadcasted_iota(
        jnp.int32, (slots, slots), 1
    )
    node_id = lax.broadcasted_iota(jnp.int32, (slots, nodes), 1).astype(F32)
    for block in range(owners):
        line = jnp.broadcast_to(sends_ref[0, block : block + 1, :].astype(F32), (slots, slots))
        column = jnp.sum(jnp.where(eye, line, 0.0), axis=1, keepdims=True)
        table[block * slots : (block + 1) * slots, :] = jnp.where(column == node_id, 1.0, 0.0)

    load_wm.wait()
    chosen = nn_dot(table[...].astype(BF16), latent_ref[0]).astype(BF16)
    projected = nn_dot(chosen, wm[...]).astype(BF16).astype(F32)
    outgoing[...] = projected.reshape(owners, slots, width)

    pl.semaphore_wait(barrier, owners - 1 + pairs - 1 + 1)

    def out_copy(step):
        return pltpu.make_async_remote_copy(
            src_ref=outgoing.at[grid_peer(step)],
            dst_ref=received.at[zi],
            send_sem=out_send.at[step],
            recv_sem=out_recv.at[step],
            device_id={"grid": grid_peer(step)},
            device_id_type=MESH,
        )

    def out_arrival(step):
        origin = lax.rem(zi + owners - step, owners)
        return pltpu.make_async_remote_copy(
            src_ref=outgoing.at[origin],
            dst_ref=received.at[origin],
            send_sem=out_send.at[step],
            recv_sem=out_recv.at[step],
            device_id={"grid": origin},
            device_id_type=MESH,
        )

    for step in range(owners - 1, 0, -1):
        out_copy(step).start()
    received[zi] = outgoing[zi]

    depth = terms.shape[0]
    for edge in range(edges):
        slot_id = lax.broadcasted_iota(jnp.int32, (rows_in, points), 0)
        hot = jnp.where(slot_id == src_ref[edge : edge + 1, :], 1.0, 0.0)
        picks[edge] = hot.astype(BF16)
        value = feat_ref[:, edge, :]
        high = value.astype(BF16).astype(F32)
        rest = value - high
        parts = [hot, high, rest, high, rest]
        parts.append(jnp.zeros((depth - rows_in - 4 * feats, points), F32))
        picks_t[edge] = jnp.concatenate(parts, axis=0).T.astype(BF16)
    embed = embed_ref[...] * 0.5
    high = embed.astype(BF16).astype(F32)
    rest = embed - high
    tail = [high, high, rest, rest]
    tail.append(jnp.zeros((depth - rows_in - 4 * feats, width), F32))
    terms[rows_in:, :] = jnp.concatenate(tail, axis=0).astype(BF16)
    ens[mi] = jnp.zeros(ens.shape[1:], BF16)
    slot[...] = jnp.zeros(slot.shape, F32)

    for step in range(1, owners):
        out_arrival(step).wait_recv()
    terms[:rows_in, :] = (received[...].reshape(rows_in, width) * 0.5).astype(BF16)
    load_wn.wait()

    def cross_copy(step, c):
        return pltpu.make_async_remote_copy(
            src_ref=ens.at[mi, c],
            dst_ref=ens.at[mi, c],
            send_sem=cross_send.at[step, c],
            recv_sem=cross_recv.at[step, c],
            device_id={"member": member_peer(step)},
            device_id_type=MESH,
        )

    def origin_of(step, side):
        return lax.rem(hi + pairs - step, pairs) * 2 + side

    def cross_arrival(step, c):
        origin = origin_of(step, lo)
        return pltpu.make_async_remote_copy(
            src_ref=ens.at[origin, c],
            dst_ref=ens.at[origin, c],
            send_sem=cross_send.at[step, c],
            recv_sem=cross_recv.at[step, c],
            device_id={"member": origin},
            device_id_type=MESH,
        )

    def sib_copy(step, c, side):
        held = ens.at[origin_of(step, side), c]
        return pltpu.make_async_remote_copy(
            src_ref=held,
            dst_ref=held,
            send_sem=sib_send.at[step, c],
            recv_sem=sib_recv.at[step, c],
            device_id={"member": sibling},
            device_id_type=MESH,
        )

    def pass_on(c):
        for step in range(1, pairs):
            cross_arrival(step, c).wait_recv()
            sib_copy(step, c, lo).start()

    def forward(c, carry):
        span = pl.ds(pl.multiple_of(c * CHUNK, CHUNK), CHUNK)
        for tile in tiles:
            total = None
            for edge in range(edges):
                half = nn_dot(picks_t[edge, span, :], terms[:, tile])
                th = jnp.tanh(half)
                bent = half * th
                act = half + bent
                total = act if total is None else total + act
                edge_slope[edge, span, tile] = ((th + 1.0) + (half - bent * th)).astype(BF16)
            hid[:, tile] = (total * (1.0 / edges)).astype(BF16)
        for tile in tiles:
            half = nn_dot(hid[...], wn[:, tile]) * 0.5
            th = jnp.tanh(half)
            bent = half * th
            mix_slope[span, tile] = ((th + 1.0) + (half - bent * th)) * 0.5
            outr[:, tile] = (hid[:, tile].astype(F32) + (half + bent)).astype(BF16)
        ens[mi, c, :variables, :] = nt_dot(wo_ref[...], outr[...]).astype(BF16)
        for step in range(1, pairs):
            cross_copy(step, c).start()
        sib_copy(0, c, lo).start()

        @pl.when(c > 0)
        def _():
            pass_on(c - 1)

        return carry

    lax.fori_loop(0, chunks, forward, 0)

    eps = softness * softness

    def backward(c, carry):
        span = pl.ds(pl.multiple_of(c * CHUNK, CHUNK), CHUNK)
        for step in range(pairs):
            sib_copy(step, c, 1 - lo).wait_recv()
        own = ens[mi, c, :variables, :].astype(F32)
        spread = jnp.zeros(own.shape, F32)
        for member in range(members):
            gap = own - ens[member, c, :variables, :].astype(F32)
            spread = spread + gap * lax.rsqrt(gap * gap + eps)
        gap = own - target_ref[:, span].astype(F32)
        slope = gap * lax.rsqrt(gap * gap + eps) * (1.0 / members) - spread * (
            1.0 / (members * (members - 1))
        )
        gp = (area_ref[:, span] * slope).astype(BF16)
        for tile in tiles:
            go = tn_dot(gp, wo_ref[:, tile])
            go_scr[:, tile] = go
            gm_scr[:, tile] = (go * mix_slope[span, tile]).astype(BF16)
        for tile in tiles:
            gh = go_scr[:, tile] + nt_dot(gm_scr[...], wn[tile, :])
            gh = gh * (0.5 / edges)
            add = None
            for edge in range(edges):
                eg = (gh * edge_slope[edge, span, tile].astype(F32)).astype(BF16)
                part = nn_dot(picks[edge, :, span], eg)
                add = part if add is None else add + part
            slot[:, tile] += add

        @pl.when(c == 0)
        def _():
            pass_on(chunks - 1)

        return carry

    lax.fori_loop(0, chunks, backward, 0)

    back[...] = slot[...].astype(BF16).astype(F32).reshape(owners, slots, width)

    def back_copy(step):
        return pltpu.make_async_remote_copy(
            src_ref=back.at[grid_peer(step)],
            dst_ref=returned.at[zi],
            send_sem=back_send.at[step],
            recv_sem=back_recv.at[step],
            device_id={"grid": grid_peer(step)},
            device_id_type=MESH,
        )

    def back_arrival(step):
        origin = lax.rem(zi + owners - step, owners)
        return pltpu.make_async_remote_copy(
            src_ref=back.at[origin],
            dst_ref=returned.at[origin],
            send_sem=back_send.at[step],
            recv_sem=back_recv.at[step],
            device_id={"grid": origin},
            device_id_type=MESH,
        )

    for step in range(owners - 1, 0, -1):
        back_copy(step).start()
    returned[zi] = back[zi]

    def score(c, carry):
        span = pl.ds(pl.multiple_of(c * CHUNK, CHUNK), CHUNK)
        truth = target_ref[:, span].astype(F32)
        values = [ens[member, c, :variables, :].astype(F32) for member in range(members)]
        skill = jnp.zeros(truth.shape, F32)
        spread = jnp.zeros(truth.shape, F32)
        for a in range(members):
            gap = values[a] - truth
            skill = skill + jnp.sqrt(gap * gap + eps)
            for b in range(a):
                gap = values[a] - values[b]
                spread = spread + jnp.sqrt(gap * gap + eps)
        crps = skill * (1.0 / members) - spread * (1.0 / (members * (members - 1)))
        mean = jnp.sum(crps, axis=0, keepdims=True) * (1.0 / variables)
        score_ref[:, span] = area_ref[:, span] * mean
        return carry

    lax.fori_loop(0, chunks, score, 0)

    for step in range(1, owners):
        back_arrival(step).wait_recv()
    gathered = returned[...].reshape(rows_in, width).astype(BF16)
    row_grad = tn_dot(table[...].astype(BF16), gathered).astype(BF16)
    grad_ref[0] = nt_dot(row_grad, wm[...]).astype(BF16)

    for step in range(1, owners):
        out_copy(step).wait_send()
        back_copy(step).wait_send()

    def drain(c, carry):
        for step in range(1, pairs):
            cross_copy(step, c).wait_send()
        for step in range(pairs):
            sib_copy(step, c, lo).wait_send()
        return carry

    lax.fori_loop(0, chunks, drain, 0)


def per_device(members, owners, latent, w_message, edge_embed, w_node, w_output, send_list, edge_src, edge_feat, cell_area, target):
    nodes, width = latent.shape[1:]
    edges, points = edge_src.shape
    feats = edge_feat.shape[0]
    slots = send_list.shape[2]
    variables = w_output.shape[0]
    rows_in = owners * slots
    depth = rup(rows_in + 4 * feats, 128)
    chunks = points // CHUNK
    padded = rup(variables, 16)
    pairs = members // 2
    vmem = pl.BlockSpec(memory_space=pltpu.VMEM)
    hbm = pl.BlockSpec(memory_space=pl.ANY)
    dma = pltpu.SemaphoreType.DMA
    latent_grad, score = pl.pallas_call(
        functools.partial(kernel, members, owners),
        out_shape=(
            jax.ShapeDtypeStruct((1, nodes, width), BF16),
            jax.ShapeDtypeStruct((1, points), F32),
        ),
        in_specs=[vmem, hbm, vmem, hbm, vmem, vmem, vmem, vmem, vmem, vmem],
        out_specs=(vmem, vmem),
        scratch_shapes=[
            pltpu.VMEM((width, width), BF16),
            pltpu.VMEM((width, width), BF16),
            pltpu.VMEM((rows_in, nodes), F32),
            pltpu.VMEM((owners, slots, width), F32),
            pltpu.VMEM((owners, slots, width), F32),
            pltpu.VMEM((owners, slots, width), F32),
            pltpu.VMEM((owners, slots, width), F32),
            pltpu.VMEM((edges, rows_in, points), BF16),
            pltpu.VMEM((edges, points, depth), BF16),
            pltpu.VMEM((depth, width), BF16),
            pltpu.VMEM((16, 128), F32),
            pltpu.VMEM((CHUNK, width), BF16),
            pltpu.VMEM((CHUNK, width), BF16),
            pltpu.VMEM((edges, points, width), BF16),
            pltpu.VMEM((points, width), F32),
            pltpu.VMEM((CHUNK, width), F32),
            pltpu.VMEM((CHUNK, width), BF16),
            pltpu.VMEM((members, chunks, padded, CHUNK), BF16),
            pltpu.VMEM((rows_in, width), F32),
            dma((2,)),
            dma((owners,)),
            dma((owners,)),
            dma((owners,)),
            dma((owners,)),
            dma((pairs, chunks)),
            dma((pairs, chunks)),
            dma((pairs, chunks)),
            dma((pairs, chunks)),
        ],
        compiler_params=pltpu.CompilerParams(
            collective_id=0, has_side_effects=True, vmem_limit_bytes=48 * 1024 * 1024
        ),
    )(
        latent,
        w_message,
        edge_embed,
        w_node,
        w_output,
        send_list,
        edge_src,
        edge_feat,
        cell_area.reshape(1, points),
        target,
    )
    return latent_grad, score.reshape(points)


def solution(mesh):
    return jax.shard_map(
        functools.partial(per_device, mesh.shape["member"], mesh.shape["grid"]),
        mesh=mesh,
        in_specs=(
            P(("groups", "member"), "grid", None),
            P(),
            P(),
            P(),
            P(),
            P("grid", None, None),
            P(None, "grid"),
            P(None, None, "grid"),
            P("grid"),
            P(None, ("groups", "grid")),
        ),
        out_specs=(P(("groups", "member"), "grid", None), P(("groups", "grid"))),
        check_vma=False,
    )
```

time: 85.1 us -> 47.9 us (0.56)
  Pallas kernels: 0 us -> 35.9 us
  matrix products: 24.3 us -> 0 us
  other arithmetic: 16.1 us -> 0 us
  local copies, waits for them, and re-layouts: 21.3 us -> 10.8 us
  starting transfers between devices: 9.6 us -> 0 us
  blocking collectives: 9.26 us -> 0 us
  waiting for transfers between devices: 2.94 us -> 0 us
    pallas_call x0 -> x1, Pallas kernels: none -> 35.9 us  [per_device(): pl.pallas_call(functools.partial(kernel, members, owners), out_shape=(jax...]
    dot_general x9 -> x0, matrix products: 24.3 us -> none  [the longest x3 10.2 us: decode_backward(): lax.dot_general(table, edge_grad, (((0,), (0,)), ((), ())), preferred_ele...]
    gather x3 -> x0, local copies, waits for them, and re-layouts: 16 us -> none  [decode_forward(): looked = jnp.take(received, sources[edge], axis=0).astype(jnp.float32)]
    unnamed x20 -> x21, local copies, waits for them, and re-layouts: 0.38 us -> 10.8 us
    convert_element_type x2 -> x0, other arithmetic: 9.85 us -> none  [the longest x1 9.66 us: decode_forward(): hidden = (summed / K).astype(jnp.bfloat16)]
    all_to_all x2 -> x0, starting transfers between devices: 9.6 us -> none  [the longest x1 6.32 us: per_device(): lax.all_to_all(outgoing, 'grid', split_axis=0, concat_axis=0, tiled=True)]
    all_gather x1 -> x0, blocking collectives: 9.26 us -> none  [per_device(): lax.all_gather(predicted[None], 'member', axis=0, tiled=True)]
    reduce_sum x2 -> x0, other arithmetic: 5.59 us -> none  [the longest x1 4.86 us: score_terms(): jnp.sum(smooth_abs(ensemble[member][None] - ensemble), axis=0)]
  transfers between devices with their start and end apart: 2 -> 0, of which waited for: 1 -> 0; matrix products, arithmetic and copies ran while one was open for 11% -> 0% of each run, Pallas kernels for 0% -> 0%
where the time goes in v1:
time: 47.9 us; the launch traced here: 47.4 us
  Pallas kernels  35.9 us (75%)
  local copies, waits for them, and re-layouts  10.8 us (23%)
  between operations  0.66 us (1%)
    pallas_call x1, Pallas kernels, per_device(): pl.pallas_call(functools.partial(kernel, members, owners), out_shape=(jax...  35.9 us
    unnamed x21, local copies, waits for them, and re-layouts  10.8 us

profile of v1, /device:TPU:0, one launch (start us, length us, event | category | flops | bytes accessed | tf_op | source)
XLA Modules:
  0.0 47.4 jit_solution(15325549792654929587)
XLA Ops:
  0.6 0.8 %copy.12.feat_ref = f32[4,3,1024]{2,1,0:T(4,128)S(1)} copy(f32[4,3,1024]{2,0,1:T(4,128)} %param.17) | data formatting | bytes 98304 | tf_op args[7]
  1.5 0.0 copy-start
  1.5 1.6 %copy-done = bf16[1024,1024]{1,0:T(8,128)(2,1)S(1)} copy-done((bf16[1024,1024]{1,0:T(8,128)(2,1)S(1)}, bf16[1024,1024]{1,0:T(8,128)(2,1)}, u32[]{:S(2)}) %copy-start) | copy-done | bytes 2097176
  3.1 0.0 copy-start.1
  3.1 1.6 %copy-done.1 = bf16[1024,1024]{1,0:T(8,128)(2,1)S(1)} copy-done((bf16[1024,1024]{1,0:T(8,128)(2,1)S(1)}, bf16[1024,1024]{1,0:T(8,128)(2,1)}, u32[]{:S(2)}) %copy-start.1) | copy-done | bytes 2097176
  4.7 0.0 copy-start.2
  4.7 0.9 %copy-done.2 = bf16[100,1024]{1,0:T(8,128)(2,1)S(1)} copy-done((bf16[100,1024]{1,0:T(8,128)(2,1)S(1)}, bf16[100,1024]{1,0:T(8,128)(2,1)}, u32[]{:S(2)}) %copy-start.2) | copy-done | bytes 204824
  5.6 0.0 copy-start.3
  5.6 0.9 %copy-done.3 = bf16[100,1024]{1,0:T(8,128)(2,1)S(1)} copy-done((bf16[100,1024]{1,0:T(8,128)(2,1)S(1)}, bf16[100,1024]{1,0:T(8,128)(2,1)}, u32[]{:S(2)}) %copy-start.3) | copy-done | bytes 204824
  6.5 0.0 copy-start.4
  6.5 0.9 %copy-done.4 = bf16[1,64,1024]{2,1,0:T(8,128)(2,1)S(1)} copy-done((bf16[1,64,1024]{2,1,0:T(8,128)(2,1)S(1)}, bf16[1,64,1024]{2,1,0:T(8,128)(2,1)}, u32[]{:S(2)}) %copy-start.4) | copy-done | bytes 131096
  7.4 0.0 copy-start.5
  7.4 0.7 %copy-done.5 = f32[4,1024]{1,0:T(4,128)S(1)} copy-done((f32[4,1024]{1,0:T(4,128)S(1)}, f32[4,1024]{1,0:T(4,128)}, u32[]{:S(2)}) %copy-start.5) | copy-done | bytes 16408
  8.1 0.0 copy-start.6
  8.1 0.7 %copy-done.6 = s32[3,1024]{1,0:T(4,128)S(1)} copy-done((s32[3,1024]{1,0:T(4,128)S(1)}, s32[3,1024]{1,0:T(4,128)}, u32[]{:S(2)}) %copy-start.6) | copy-done | bytes 12312
  8.9 0.0 copy-start.7
  8.9 0.7 %copy-done.7 = f32[1024]{0:T(1024)S(1)} copy-done((f32[1024]{0:T(1024)S(1)}, f32[1024]{0:T(1024)}, u32[]{:S(2)}) %copy-start.7) | copy-done | bytes 4120
  9.5 0.0 copy-start.8
  9.5 0.7 %copy-done.8 = s32[1,4,8]{2,1,0:T(4,128)S(1)} copy-done((s32[1,4,8]{2,1,0:T(4,128)S(1)}, s32[1,4,8]{2,1,0:T(4,128)}, u32[]{:S(2)}) %copy-start.8) | copy-done | bytes 152
  10.2 35.9 %shard_map.113 = (bf16[1,64,1024]{2,1,0:T(8,128)(2,1)S(1)}, f32[1,1024]{1,0:T(1,128)S(1)}) custom-call(bf16[1,64,1024]{2,1,0:T(8,128)(2,1)S(1)} %copy-done.4, bf16[1024,1024]{1,0:T(8,128)(2,1)S(1)} %copy-done, f32[4,1024]{1,0:T(4,128)S(1)} %copy-done.5, bf16[1024,1024]{1,0:T(8,128)(2,1)S(1)} %copy-done.1, bf16[100,1024]{1,0:T(8,128)(2,1)S(1)} %copy-done.2, ...), custom_call_target="tpu_custom_call" | custom-call | tf_op jit(solution)/shard_map/pallas_call | solution.py:372
  46.1 0.7 %copy.15 = bf16[1,64,1024]{2,1,0:T(8,128)(2,1)} copy(bf16[1,64,1024]{2,1,0:T(8,128)(2,1)S(1)} %get-tuple-element.8) | data formatting | bytes 262144
  46.8 0.6 %copy.16 = f32[1024]{0:T(1024)} copy(f32[1024]{0:T(1024)S(1)} %bitcast.3) | data formatting | bytes 8192
Async XLA Ops:
  1.5 1.6 %copy-start = (bf16[1024,1024]{1,0:T(8,128)(2,1)S(1)}, bf16[1024,1024]{1,0:T(8,128)(2,1)}, u32[]{:S(2)}) copy-start(bf16[1024,1024]{1,0:T(8,128)(2,1)} %wm_hbm.1) | copy-start | bytes 6291460
  3.1 1.6 %copy-start.1 = (bf16[1024,1024]{1,0:T(8,128)(2,1)S(1)}, bf16[1024,1024]{1,0:T(8,128)(2,1)}, u32[]{:S(2)}) copy-start(bf16[1024,1024]{1,0:T(8,128)(2,1)} %wn_hbm.1) | copy-start | bytes 6291460
  4.7 0.9 %copy-start.2 = (bf16[100,1024]{1,0:T(8,128)(2,1)S(1)}, bf16[100,1024]{1,0:T(8,128)(2,1)}, u32[]{:S(2)}) copy-start(bf16[100,1024]{1,0:T(8,128)(2,1)} %wo_ref.1) | copy-start | bytes 614404
  5.6 0.9 %copy-start.3 = (bf16[100,1024]{1,0:T(8,128)(2,1)S(1)}, bf16[100,1024]{1,0:T(8,128)(2,1)}, u32[]{:S(2)}) copy-start(bf16[100,1024]{1,0:T(8,128)(2,1)} %target_ref.1) | copy-start | bytes 614404
  6.5 0.9 %copy-start.4 = (bf16[1,64,1024]{2,1,0:T(8,128)(2,1)S(1)}, bf16[1,64,1024]{2,1,0:T(8,128)(2,1)}, u32[]{:S(2)}) copy-start(bf16[1,64,1024]{2,1,0:T(8,128)(2,1)} %latent_ref.1) | copy-start | bytes 393220
  7.4 0.7 %copy-start.5 = (f32[4,1024]{1,0:T(4,128)S(1)}, f32[4,1024]{1,0:T(4,128)}, u32[]{:S(2)}) copy-start(f32[4,1024]{1,0:T(4,128)} %embed_ref.1) | copy-start | bytes 49156
  8.1 0.7 %copy-start.6 = (s32[3,1024]{1,0:T(4,128)S(1)}, s32[3,1024]{1,0:T(4,128)}, u32[]{:S(2)}) copy-start(s32[3,1024]{1,0:T(4,128)} %src_ref.1) | copy-start | bytes 36868
  8.9 0.7 %copy-start.7 = (f32[1024]{0:T(1024)S(1)}, f32[1024]{0:T(1024)}, u32[]{:S(2)}) copy-start(f32[1024]{0:T(1024)} %param.18) | copy-start | bytes 12292
  9.5 0.7 %copy-start.8 = (s32[1,4,8]{2,1,0:T(4,128)S(1)}, s32[1,4,8]{2,1,0:T(4,128)}, u32[]{:S(2)}) copy-start(s32[1,4,8]{2,1,0:T(4,128)} %sends_ref.1) | copy-start | bytes 388

commit v2 on v1

--- a/solution.py
+++ b/solution.py
@@ -12,16 +12,26 @@
 MESH = pl.DeviceIdType.MESH
 
 softness = 0.1
-CHUNK = 256
-TILE = 256
+CHUNK = 512
+TILE = 512
 
 
 def rup(value, unit):
     return (value + unit - 1) // unit * unit
 
 
-def nt_dot(a, b):
-    return lax.dot_general(a, b, (((1,), (1,)), ((), ())), preferred_element_type=F32)
+def fold(rows, owners):
+    slots, width = rows.shape[0] // owners, rows.shape[1]
+    split = rows.reshape(owners, slots, width)
+    halves = [split[:, :, : width // 2], split[:, :, width // 2 :]]
+    return jnp.concatenate(halves, axis=1).astype(BF16)
+
+
+def unfold(blocks):
+    wide = blocks.astype(F32)
+    owners, slots, half = wide.shape[0], wide.shape[1] // 2, wide.shape[2]
+    halves = [wide[:, :slots, :], wide[:, slots:, :]]
+    return jnp.concatenate(halves, axis=2).reshape(owners * slots, 2 * half)
 
 
 def tn_dot(a, b):
@@ -35,20 +45,28 @@
 def kernel(
     members,
     owners,
+    latent_hbm,
+    wm_hbm,
+    embed_hbm,
+    wn_hbm,
+    wo_hbm,
+    sends_hbm,
+    src_hbm,
+    feat_hbm,
+    area_hbm,
+    target_hbm,
+    grad_ref,
+    score_ref,
     latent_ref,
-    wm_hbm,
+    wm,
     embed_ref,
-    wn_hbm,
+    wn,
     wo_ref,
     sends_ref,
     src_ref,
     feat_ref,
     area_ref,
     target_ref,
-    grad_ref,
-    score_ref,
-    wm,
-    wn,
     table,
     outgoing,
     received,
@@ -57,7 +75,6 @@
     picks,
     picks_t,
     terms,
-    low,
     hid,
     outr,
     edge_slope,
@@ -66,6 +83,10 @@
     gm_scr,
     ens,
     slot,
+    wn_t,
+    wm_t,
+    wo_wide,
+    wo_t,
     local_sem,
     out_send,
     out_recv,
@@ -79,7 +100,7 @@
     width = latent_ref.shape[2]
     nodes = latent_ref.shape[1]
     edges, points = src_ref.shape
-    feats = feat_ref.shape[0]
+    feats = feat_ref.shape[1]
     slots = sends_ref.shape[2]
     variables = wo_ref.shape[0]
     rows_in = owners * slots
@@ -92,10 +113,25 @@
     hi, lo = lax.div(mi, 2), lax.rem(mi, 2)
     sibling = hi * 2 + 1 - lo
 
-    load_wm = pltpu.make_async_copy(wm_hbm, wm, local_sem.at[0])
-    load_wn = pltpu.make_async_copy(wn_hbm, wn, local_sem.at[1])
-    load_wm.start()
-    load_wn.start()
+    loads = [
+        pltpu.make_async_copy(source, held, local_sem.at[which])
+        for which, (source, held) in enumerate(
+            [
+                (sends_hbm, sends_ref),
+                (latent_hbm, latent_ref),
+                (wm_hbm, wm),
+                (src_hbm, src_ref),
+                (feat_hbm, feat_ref),
+                (embed_hbm, embed_ref),
+                (wn_hbm, wn),
+                (wo_hbm, wo_ref),
+                (area_hbm, area_ref),
+                (target_hbm, target_ref),
+            ]
+        )
+    ]
+    for load in loads:
+        load.start()
 
     def grid_peer(step):
         return lax.rem(zi + step, owners)
@@ -114,6 +150,7 @@
         )
     pl.semaphore_signal(barrier, inc=1, device_id={"member": sibling}, device_id_type=MESH)
 
+    loads[0].wait()
     eye = lax.broadcasted_iota(jnp.int32, (slots, slots), 0) == lax.broadcasted_iota(
         jnp.int32, (slots, slots), 1
     )
@@ -123,10 +160,8 @@
         column = jnp.sum(jnp.where(eye, line, 0.0), axis=1, keepdims=True)
         table[block * slots : (block + 1) * slots, :] = jnp.where(column == node_id, 1.0, 0.0)
 
-    load_wm.wait()
-    chosen = nn_dot(table[...].astype(BF16), latent_ref[0]).astype(BF16)
-    projected = nn_dot(chosen, wm[...]).astype(BF16).astype(F32)
-    outgoing[...] = projected.reshape(owners, slots, width)
+    loads[1].wait()
+    outgoing[...] = fold(nn_dot(table[...].astype(BF16), latent_ref[0]), owners)
 
     pl.semaphore_wait(barrier, owners - 1 + pairs - 1 + 1)
 
@@ -155,12 +190,14 @@
         out_copy(step).start()
     received[zi] = outgoing[zi]
 
+    for load in loads[3:6]:
+        load.wait()
     depth = terms.shape[0]
     for edge in range(edges):
         slot_id = lax.broadcasted_iota(jnp.int32, (rows_in, points), 0)
         hot = jnp.where(slot_id == src_ref[edge : edge + 1, :], 1.0, 0.0)
         picks[edge] = hot.astype(BF16)
-        value = feat_ref[:, edge, :]
+        value = feat_ref[edge]
         high = value.astype(BF16).astype(F32)
         rest = value - high
         parts = [hot, high, rest, high, rest]
@@ -172,13 +209,22 @@
     tail = [high, high, rest, rest]
     tail.append(jnp.zeros((depth - rows_in - 4 * feats, width), F32))
     terms[rows_in:, :] = jnp.concatenate(tail, axis=0).astype(BF16)
-    ens[mi] = jnp.zeros(ens.shape[1:], BF16)
     slot[...] = jnp.zeros(slot.shape, F32)
+    for load in loads[6:]:
+        load.wait()
+    for tile in tiles:
+        wn_t[:, tile] = wn[tile, :].T
+    wo_wide[...] = jnp.zeros(wo_wide.shape, F32)
+    wo_wide[:variables, :] = wo_ref[...].astype(F32)
+    wo_t[...] = wo_wide[...].T.astype(BF16)
+    loads[2].wait()
 
     for step in range(1, owners):
         out_arrival(step).wait_recv()
-    terms[:rows_in, :] = (received[...].reshape(rows_in, width) * 0.5).astype(BF16)
-    load_wn.wait()
+    projected = nn_dot(unfold(received[...]).astype(BF16), wm[...]).astype(BF16).astype(F32)
+    terms[:rows_in, :] = (projected * 0.5).astype(BF16)
+    for tile in tiles:
+        wm_t[:, tile] = wm[tile, :].T
 
     def cross_copy(step, c):
         return pltpu.make_async_remote_copy(
@@ -220,25 +266,33 @@
             cross_arrival(step, c).wait_recv()
             sib_copy(step, c, lo).start()
 
-    def forward(c, carry):
+    def edge_tile(c, tile):
         span = pl.ds(pl.multiple_of(c * CHUNK, CHUNK), CHUNK)
-        for tile in tiles:
-            total = None
-            for edge in range(edges):
-                half = nn_dot(picks_t[edge, span, :], terms[:, tile])
-                th = jnp.tanh(half)
-                bent = half * th
-                act = half + bent
-                total = act if total is None else total + act
-                edge_slope[edge, span, tile] = ((th + 1.0) + (half - bent * th)).astype(BF16)
-            hid[:, tile] = (total * (1.0 / edges)).astype(BF16)
-        for tile in tiles:
-            half = nn_dot(hid[...], wn[:, tile]) * 0.5
+        total = None
+        for edge in range(edges):
+            half = nn_dot(picks_t[edge, span, :], terms[:, tile])
             th = jnp.tanh(half)
             bent = half * th
-            mix_slope[span, tile] = ((th + 1.0) + (half - bent * th)) * 0.5
-            outr[:, tile] = (hid[:, tile].astype(F32) + (half + bent)).astype(BF16)
-        ens[mi, c, :variables, :] = nt_dot(wo_ref[...], outr[...]).astype(BF16)
+            act = half + bent
+            total = act if total is None else total + act
+            edge_slope[edge, span, tile] = ((th + 1.0) + (half - bent * th)).astype(BF16)
+        hid[0, :, tile] = (total * (1.0 / edges)).astype(BF16)
+
+    def mix_tile(c, tile):
+        span = pl.ds(pl.multiple_of(c * CHUNK, CHUNK), CHUNK)
+        half = nn_dot(hid[0], wn[:, tile]) * 0.5
+        th = jnp.tanh(half)
+        bent = half * th
+        mix_slope[span, tile] = ((th + 1.0) + (half - bent * th)) * 0.5
+        outr[0, :, tile] = (hid[0, :, tile].astype(F32) + (half + bent)).astype(BF16)
+
+    def forward(c, carry):
+        for tile in tiles:
+            edge_tile(c, tile)
+        for tile in tiles:
+            mix_tile(c, tile)
+        guess = nn_dot(outr[0], wo_t[...]).T
+        ens[mi, c] = guess[: ens.shape[2], :].astype(BF16)
         for step in range(1, pairs):
             cross_copy(step, c).start()
         sib_copy(0, c, lo).start()
@@ -253,7 +307,7 @@
 
     eps = softness * softness
 
-    def backward(c, carry):
+    def lead(c):
         span = pl.ds(pl.multiple_of(c * CHUNK, CHUNK), CHUNK)
         for step in range(pairs):
             sib_copy(step, c, 1 - lo).wait_recv()
@@ -266,20 +320,31 @@
         slope = gap * lax.rsqrt(gap * gap + eps) * (1.0 / members) - spread * (
             1.0 / (members * (members - 1))
         )
-        gp = (area_ref[:, span] * slope).astype(BF16)
+        return (area_ref[:, span] * slope).astype(BF16)
+
+    def lead_tile(c, gp, tile):
+        span = pl.ds(pl.multiple_of(c * CHUNK, CHUNK), CHUNK)
+        go = tn_dot(gp, wo_ref[:, tile])
+        go_scr[0, :, tile] = go
+        gm_scr[0, :, tile] = (go * mix_slope[span, tile]).astype(BF16)
+
+    def edge_back(c, tile):
+        span = pl.ds(pl.multiple_of(c * CHUNK, CHUNK), CHUNK)
+        gh = go_scr[0, :, tile] + nn_dot(gm_scr[0], wn_t[:, tile])
+        gh = gh * (0.5 / edges)
+        add = None
+        for edge in range(edges):
+            eg = (gh * edge_slope[edge, span, tile].astype(F32)).astype(BF16)
+            part = nn_dot(picks[edge, :, span], eg)
+            add = part if add is None else add + part
+        slot[:, tile] += add
+
+    def backward(c, carry):
+        gp = lead(c)
         for tile in tiles:
-            go = tn_dot(gp, wo_ref[:, tile])
-            go_scr[:, tile] = go
-            gm_scr[:, tile] = (go * mix_slope[span, tile]).astype(BF16)
+            lead_tile(c, gp, tile)
         for tile in tiles:
-            gh = go_scr[:, tile] + nt_dot(gm_scr[...], wn[tile, :])
-            gh = gh * (0.5 / edges)
-            add = None
-            for edge in range(edges):
-                eg = (gh * edge_slope[edge, span, tile].astype(F32)).astype(BF16)
-                part = nn_dot(picks[edge, :, span], eg)
-                add = part if add is None else add + part
-            slot[:, tile] += add
+            edge_back(c, tile)
 
         @pl.when(c == 0)
         def _():
@@ -289,7 +354,7 @@
 
     lax.fori_loop(0, chunks, backward, 0)
 
-    back[...] = slot[...].astype(BF16).astype(F32).reshape(owners, slots, width)
+    back[...] = fold(slot[...], owners)
 
     def back_copy(step):
         return pltpu.make_async_remote_copy(
@@ -324,10 +389,12 @@
         spread = jnp.zeros(truth.shape, F32)
         for a in range(members):
             gap = values[a] - truth
-            skill = skill + jnp.sqrt(gap * gap + eps)
+            gap = gap * gap + eps
+            skill = skill + gap * lax.rsqrt(gap)
             for b in range(a):
                 gap = values[a] - values[b]
-                spread = spread + jnp.sqrt(gap * gap + eps)
+                gap = gap * gap + eps
+                spread = spread + gap * lax.rsqrt(gap)
         crps = skill * (1.0 / members) - spread * (1.0 / (members * (members - 1)))
         mean = jnp.sum(crps, axis=0, keepdims=True) * (1.0 / variables)
         score_ref[:, span] = area_ref[:, span] * mean
@@ -337,9 +404,9 @@
 
     for step in range(1, owners):
         back_arrival(step).wait_recv()
-    gathered = returned[...].reshape(rows_in, width).astype(BF16)
+    gathered = unfold(returned[...]).astype(BF16)
     row_grad = tn_dot(table[...].astype(BF16), gathered).astype(BF16)
-    grad_ref[0] = nt_dot(row_grad, wm[...]).astype(BF16)
+    grad_ref[0] = nn_dot(row_grad, wm_t[...]).astype(BF16)
 
     for step in range(1, owners):
         out_copy(step).wait_send()
@@ -359,6 +426,8 @@
     nodes, width = latent.shape[1:]
     edges, points = edge_src.shape
     feats = edge_feat.shape[0]
+    edge_feat = jnp.transpose(edge_feat, (1, 0, 2))
+    cell_area = cell_area.reshape(1, points)
     slots = send_list.shape[2]
     variables = w_output.shape[0]
     rows_in = owners * slots
@@ -366,38 +435,52 @@
     chunks = points // CHUNK
     padded = rup(variables, 16)
     pairs = members // 2
+    arrays = (
+        latent,
+        w_message,
+        edge_embed,
+        w_node,
+        w_output,
+        send_list,
+        edge_src,
+        edge_feat,
+        cell_area,
+        target,
+    )
     vmem = pl.BlockSpec(memory_space=pltpu.VMEM)
-    hbm = pl.BlockSpec(memory_space=pl.ANY)
+    hbm = pl.BlockSpec(memory_space=pltpu.HBM)
     dma = pltpu.SemaphoreType.DMA
     latent_grad, score = pl.pallas_call(
         functools.partial(kernel, members, owners),
         out_shape=(
-            jax.ShapeDtypeStruct((1, nodes, width), BF16),
-            jax.ShapeDtypeStruct((1, points), F32),
+            pltpu.VMEM((1, nodes, width), BF16),
+            pltpu.VMEM((1, points), F32),
         ),
-        in_specs=[vmem, hbm, vmem, hbm, vmem, vmem, vmem, vmem, vmem, vmem],
+        in_specs=[hbm] * 10,
         out_specs=(vmem, vmem),
         scratch_shapes=[
-            pltpu.VMEM((width, width), BF16),
-            pltpu.VMEM((width, width), BF16),
+            *[pltpu.VMEM(array.shape, array.dtype) for array in arrays],
             pltpu.VMEM((rows_in, nodes), F32),
-            pltpu.VMEM((owners, slots, width), F32),
-            pltpu.VMEM((owners, slots, width), F32),
-            pltpu.VMEM((owners, slots, width), F32),
-            pltpu.VMEM((owners, slots, width), F32),
+            pltpu.VMEM((owners, 2 * slots, width // 2), BF16),
+            pltpu.VMEM((owners, 2 * slots, width // 2), BF16),
+            pltpu.VMEM((owners, 2 * slots, width // 2), BF16),
+            pltpu.VMEM((owners, 2 * slots, width // 2), BF16),
             pltpu.VMEM((edges, rows_in, points), BF16),
             pltpu.VMEM((edges, points, depth), BF16),
             pltpu.VMEM((depth, width), BF16),
-            pltpu.VMEM((16, 128), F32),
-            pltpu.VMEM((CHUNK, width), BF16),
-            pltpu.VMEM((CHUNK, width), BF16),
+            pltpu.VMEM((2, CHUNK, width), BF16),
+            pltpu.VMEM((2, CHUNK, width), BF16),
             pltpu.VMEM((edges, points, width), BF16),
             pltpu.VMEM((points, width), F32),
-            pltpu.VMEM((CHUNK, width), F32),
-            pltpu.VMEM((CHUNK, width), BF16),
+            pltpu.VMEM((2, CHUNK, width), F32),
+            pltpu.VMEM((2, CHUNK, width), BF16),
             pltpu.VMEM((members, chunks, padded, CHUNK), BF16),
             pltpu.VMEM((rows_in, width), F32),
-            dma((2,)),
+            pltpu.VMEM((width, width), BF16),
+            pltpu.VMEM((width, width), BF16),
+            pltpu.VMEM((rup(variables, 128), width), F32),
+            pltpu.VMEM((width, rup(variables, 128)), BF16),
+            dma((len(arrays),)),
             dma((owners,)),
             dma((owners,)),
             dma((owners,)),
@@ -408,20 +491,9 @@
             dma((pairs, chunks)),
         ],
         compiler_params=pltpu.CompilerParams(
-            collective_id=0, has_side_effects=True, vmem_limit_bytes=48 * 1024 * 1024
+            collective_id=0, has_side_effects=True, vmem_limit_bytes=60 * 1024 * 1024
         ),
-    )(
-        latent,
-        w_message,
-        edge_embed,
-        w_node,
-        w_output,
-        send_list,
-        edge_src,
-        edge_feat,
-        cell_area.reshape(1, points),
-        target,
-    )
+    )(*arrays)
     return latent_grad, score.reshape(points)
 
 

time: 47.9 us -> 32.9 us (0.69)
  local copies, waits for them, and re-layouts: 10.8 us -> 1.25 us
  Pallas kernels: 35.9 us -> 30.8 us
    unnamed x21 -> x2, local copies, waits for them, and re-layouts: 10.8 us -> 1.25 us
    pallas_call x1, Pallas kernels: 35.9 us -> 30.8 us  [per_device(): pl.pallas_call(functools.partial(kernel, members, owners), out_shape=(plt...]
where the time goes in v2:
time: 32.9 us; the launch traced here: 32.7 us
  Pallas kernels  30.8 us (94%)
  local copies, waits for them, and re-layouts  1.25 us (4%)
  between operations  0.64 us (2%)
    pallas_call x1, Pallas kernels, per_device(): pl.pallas_call(functools.partial(kernel, members, owners), out_shape=(plt...  30.8 us
    unnamed x2, local copies, waits for them, and re-layouts  1.25 us

profile of v2, /device:TPU:0, one launch (start us, length us, event | category | flops | bytes accessed | tf_op | source)
XLA Modules:
  0.0 32.7 jit_solution(4090238606900626723)
XLA Ops:
  0.6 30.8 %shard_map.113 = (bf16[1,64,1024]{2,1,0:T(8,128)(2,1)S(1)}, f32[1,1024]{1,0:T(1,128)S(1)}) custom-call(bf16[1,64,1024]{2,1,0:T(8,128)(2,1)} %latent_hbm.1, bf16[1024,1024]{1,0:T(8,128)(2,1)} %wm_hbm.1, f32[4,1024]{1,0:T(4,128)} %embed_hbm.1, bf16[1024,1024]{1,0:T(8,128)(2,1)} %wn_hbm.1, bf16[100,1024]{1,0:T(8,128)(2,1)} %wo_hbm.1, s32[1,4,8]{2,1,0:T(4,128)} %sends_hbm.1, ...), custom_call_target="tpu_custom_call" | custom-call | tf_op jit(solution)/shard_map/pallas_call | solution.py:453
  31.5 0.7 %copy.14 = bf16[1,64,1024]{2,1,0:T(8,128)(2,1)} copy(bf16[1,64,1024]{2,1,0:T(8,128)(2,1)S(1)} %get-tuple-element.6) | data formatting | bytes 262144
  32.1 0.6 %copy.15 = f32[1024]{0:T(1024)} copy(f32[1024]{0:T(1024)S(1)} %bitcast.3) | data formatting | bytes 8192

commit v3 on v2

--- a/solution.py
+++ b/solution.py
@@ -14,6 +14,7 @@
 softness = 0.1
 CHUNK = 512
 TILE = 512
+NARROW = 128
 
 
 def rup(value, unit):
@@ -223,8 +224,6 @@
         out_arrival(step).wait_recv()
     projected = nn_dot(unfold(received[...]).astype(BF16), wm[...]).astype(BF16).astype(F32)
     terms[:rows_in, :] = (projected * 0.5).astype(BF16)
-    for tile in tiles:
-        wm_t[:, tile] = wm[tile, :].T
 
     def cross_copy(step, c):
         return pltpu.make_async_remote_copy(
@@ -382,9 +381,11 @@
     returned[zi] = back[zi]
 
     def score(c, carry):
-        span = pl.ds(pl.multiple_of(c * CHUNK, CHUNK), CHUNK)
+        span = pl.ds(pl.multiple_of(c * NARROW, NARROW), NARROW)
+        held = lax.div(c, CHUNK // NARROW)
+        part = pl.ds(pl.multiple_of(lax.rem(c, CHUNK // NARROW) * NARROW, NARROW), NARROW)
         truth = target_ref[:, span].astype(F32)
-        values = [ens[member, c, :variables, :].astype(F32) for member in range(members)]
+        values = [ens[member, held, :variables, part].astype(F32) for member in range(members)]
         skill = jnp.zeros(truth.shape, F32)
         spread = jnp.zeros(truth.shape, F32)
         for a in range(members):
@@ -400,7 +401,9 @@
         score_ref[:, span] = area_ref[:, span] * mean
         return carry
 
-    lax.fori_loop(0, chunks, score, 0)
+    for tile in tiles:
+        wm_t[:, tile] = wm[tile, :].T
+    lax.fori_loop(0, points // NARROW, score, 0)
 
     for step in range(1, owners):
         back_arrival(step).wait_recv()

time: 32.9 us -> 32.6 us (level)
  no operation moved by 1% of the time
where the time goes in v3:
time: 32.6 us; the launch traced here: 32.5 us
  Pallas kernels  30.6 us (94%)
  local copies, waits for them, and re-layouts  1.25 us (4%)
  between operations  0.64 us (2%)
    pallas_call x1, Pallas kernels, per_device(): pl.pallas_call(functools.partial(kernel, members, owners), out_shape=(plt...  30.6 us
    unnamed x2, local copies, waits for them, and re-layouts  1.25 us

profile of v3, /device:TPU:0, one launch (start us, length us, event | category | flops | bytes accessed | tf_op | source)
XLA Modules:
  0.0 32.5 jit_solution(1405543455445213095)
XLA Ops:
  0.6 30.6 %shard_map.113 = (bf16[1,64,1024]{2,1,0:T(8,128)(2,1)S(1)}, f32[1,1024]{1,0:T(1,128)S(1)}) custom-call(bf16[1,64,1024]{2,1,0:T(8,128)(2,1)} %latent_hbm.1, bf16[1024,1024]{1,0:T(8,128)(2,1)} %wm_hbm.1, f32[4,1024]{1,0:T(4,128)} %embed_hbm.1, bf16[1024,1024]{1,0:T(8,128)(2,1)} %wn_hbm.1, bf16[100,1024]{1,0:T(8,128)(2,1)} %wo_hbm.1, s32[1,4,8]{2,1,0:T(4,128)} %sends_hbm.1, ...), custom_call_target="tpu_custom_call" | custom-call | tf_op jit(solution)/shard_map/pallas_call | solution.py:456
  31.2 0.7 %copy.14 = bf16[1,64,1024]{2,1,0:T(8,128)(2,1)} copy(bf16[1,64,1024]{2,1,0:T(8,128)(2,1)S(1)} %get-tuple-element.6) | data formatting | bytes 262144
  31.9 0.6 %copy.15 = f32[1024]{0:T(1024)} copy(f32[1024]{0:T(1024)S(1)} %bitcast.3) | data formatting | bytes 8192
